TPU v7x, 512 devices: a whole 4x4x16 slice. The times are simulated.
512 devices in a mesh: ka: 32 (over z, x_lo), pw: 16 (over x_hi, y, core).
Axes of the slice: x: 4 (x_hi: 2, x_lo: 2; x = x_hi * 2 + x_lo), y: 4, z: 16, core: 2. Of those that a mesh axis runs over, the one named last changes fastest.
Arguments:
- wave: bfloat16 [32, 2, 256, 20480], P('ka', None, None, 'pw'), may hold values from -0.4375 to 0.4375
- wave_perm: int32 [32, 3, 20480], P('ka', None, 'pw'), may hold values from 0 to 20479, as said below
- shell_weight: float32 [3], replicated, may hold values from 0.25 to 1
Outputs:
- correlation: float32 [32, 3, 2, 256, 256], P('ka', None, None, 'pw')
- gradient: float32 [32, 2, 256, 256], P('ka')
Inputs may be any that keep to these rules, and one draw needn't show every extreme that they name: Each list wave_perm[k, d, :] is a permutation of the 20480 plane waves that maps every aligned block of 1280 rows onto itself.
All inputs are finite; a program needn't handle non-finite values.
Results may differ from a plain program's by a relative error of at most 0.0003.
Values may be sent and summed in bfloat16 or wider, within the bound.
A program may use at most 64 MiB of HBM per device.

v0:
```python
import jax
import jax.numpy as jnp
from jax import lax
from jax.experimental import pallas as pl
from jax.experimental.pallas import tpu as pltpu
from jax.sharding import PartitionSpec as P

MESH = pl.DeviceIdType.MESH
NK = 32
NB = 256
NG = 1280
NQ = 8
HOPS = 4
CHUNKS = 4
ROWS = NB // CHUNKS
BLOCKS = ROWS // 16
A, B, W, C = range(4)
BLOCK = 72
HALF = 40


def kernel(
    wave_in, wave_halves, perm, weight, corr_out, grad_out,
    wave, stream, other, turned, product, lists, part, gathered, reduced, ends, zrows,
    stream_send, stream_recv, other_send, other_recv, list_send, list_recv,
    part_send, part_recv, end_send, end_recv, z_send, z_recv, zz_send, zz_recv, wave_sem, list_sem, told,
):
    k = lax.axis_index("ka")
    p = lax.axis_index("pw")
    core = p % 2
    q = p // 2
    sibling = p + 1 - 2 * core
    level = k // 2 % 4
    group = k // 8 * 8
    inner = k % 8
    to_next = (k + 30 + 4 * core) % NK
    a_up, a_down = (k + 8) % NK, (k + 24) % NK
    b_up, b_down = group + (inner + 2) % 8, group + (inner + 6) % 8
    flip = k + 1 - 2 * (k % 2)
    a_end = (k + 8 + 16 * core) % NK
    b_end = group + (inner + 2 + 4 * core) % 8
    w_end = group + (inner + 6 - 4 * core) % 8
    b_here = level != 3 - 3 * core
    w_here = level == 3 * core

    def remote(src, dst, send_sem, recv_sem, ka, pw):
        return pltpu.make_async_remote_copy(
            src_ref=src, dst_ref=dst, send_sem=send_sem, recv_sem=recv_sem,
            device_id=(ka, pw), device_id_type=MESH,
        )

    wave_copy = pltpu.make_async_copy(wave_in, wave, wave_sem)
    own_list_copy = pltpu.make_async_copy(perm, lists.at[0], list_sem)
    wave_copy.start()
    own_list_copy.start()

    around = [
        ((k + 2) % NK, p), ((k + 30) % NK, p), (flip, p), (flip, (q + 4) % NQ * 2 + core),
        (k, (q // 4 * 4 + (q + 1) % 4) * 2 + core), (k, (q // 4 * 4 + (q + 3) % 4) * 2 + core), (k, sibling),
    ]

    def tell(sem):
        for neighbour in around:
            pl.semaphore_signal(sem, inc=1, device_id=neighbour, device_id_type=MESH)

    barrier = pltpu.get_barrier_semaphore()
    tell(barrier)
    pl.semaphore_wait(barrier, len(around))

    def blocks(c):
        return pl.ds(c * BLOCKS, BLOCKS)

    def own_copy(c, source):
        return remote(
            source, stream.at[0, :, blocks(c)],
            stream_send.at[0, c], stream_recv.at[0, c], to_next, p,
        )

    def hop_copy(h, c):
        return remote(
            stream.at[h - 1, :, blocks(c)], stream.at[h, :, blocks(c)],
            stream_send.at[h, c], stream_recv.at[h, c], to_next, p,
        )

    def list_copy(h):
        source = perm if h == 0 else lists.at[h]
        return remote(
            source.at[0:2], lists.at[h + 1, 0:2], list_send.at[h], list_recv.at[h], to_next, p
        )

    other_copy = remote(wave_in, other, other_send, other_recv, flip, p)

    list_copy(0).start()

    @pl.when(core == 0)
    def _():
        for c in range(CHUNKS):
            own_copy(c, wave_in.at[:, blocks(c)]).start()

    @pl.when(core == 1)
    def _():
        for c in range(CHUNKS):
            own_copy(c, wave_halves.at[:, c % 2 * 4:c % 2 * 4 + 4, c // 2]).start()

    other_copy.start()
    tell(told.at[0])
    own_list_copy.wait()
    wave_copy.wait()

    def turn(slot):
        which = (1 - core) * 3 * (slot // 2) * (1 - slot % 2) + core * (4 - 3 * slot) * (1 - slot // 2)
        direction = (slot + 1) // 2
        at_start = (1 - core) * (1 - slot // 2 * (1 - slot % 2)) + core * (slot // 2)

        @pl.when(at_start == 1)
        def _():
            @pl.loop(0, NG // 256)
            def _(j):
                row = lists[which, direction] - p * NG
                wanted = lax.broadcasted_iota(jnp.int32, (256, NG), 0) + j * 256
                pick = jnp.where(wanted == row, 1.0, 0.0).astype(jnp.bfloat16)
                value = lax.dot_general(
                    wave[...].reshape(2 * NB, NG), pick, (((1,), (1,)), ((), ())),
                    preferred_element_type=jnp.float32,
                )
                turned[slot, :, pl.ds(pl.multiple_of(j * 256, 256), 256)] = value.astype(jnp.bfloat16)

        @pl.when(at_start == 0)
        def _():
            @pl.loop(0, NG // 256)
            def _(j):
                columns = pl.ds(pl.multiple_of(j * 256, 256), 256)
                row = lists[which, direction, :, columns] - p * NG
                held = lax.broadcasted_iota(jnp.int32, (NG, 256), 0)
                pick = jnp.where(held == row, 1.0, 0.0).astype(jnp.bfloat16)
                value = lax.dot_general(
                    wave[...].reshape(2 * NB, NG), pick, (((1,), (0,)), ((), ())),
                    preferred_element_type=jnp.float32,
                )
                turned[slot, :, columns] = value.astype(jnp.bfloat16)

    def multiply(slot, source, c, order):
        value = lax.dot_general(
            source[:, blocks(c)].reshape(2 * ROWS, NG), turned[slot], (((1,), (1,)), ((), ())),
            preferred_element_type=jnp.float32,
        )
        real = value[:ROWS, :NB] + value[ROWS:, NB:]
        imag = value[:ROWS, NB:] - value[ROWS:, :NB]
        for i in range(BLOCKS):
            n = c * BLOCKS + i
            block = n + order * (n % NQ * 2 + n // NQ - n)
            rows = pl.ds(pl.multiple_of(block * 16, 16), 16)
            product[0, rows, :] = real[16 * i:16 * i + 16]
            product[1, rows, :] = imag[16 * i:16 * i + 16]

    def part_copy(slot, j):
        dest = (q + j) % NQ
        return remote(
            part.at[slot, dest], gathered.at[slot, j],
            part_send.at[slot, j], part_recv.at[slot, j], k, dest * 2 + core,
        )

    def hand_out(slot, at_start):
        swap = jnp.broadcast_to(at_start, (NB, NB)) > 0
        real, imag = product[0], product[1]
        real = jnp.where(swap, real.T, real)
        imag = jnp.where(swap, -imag.T, imag)
        eye = lax.broadcasted_iota(jnp.int32, (NB, NB), 0) == lax.broadcasted_iota(jnp.int32, (NB, NB), 1)
        diag_real = jnp.sum(jnp.where(eye, real, 0.0), axis=0, keepdims=True)
        diag_imag = jnp.sum(jnp.where(eye, imag, 0.0), axis=0, keepdims=True)
        first = lax.broadcasted_iota(jnp.int32, (8, NB), 0) < 4
        diag = jnp.where(first, diag_real, diag_imag)
        real = real.reshape(NQ, 2, 16, NB)
        imag = imag.reshape(NQ, 2, 16, NB)
        part[slot, :, 0:16, :] = real[:, 0]
        part[slot, :, 16:32, :] = imag[:, 0]
        part[slot, :, 32:48, :] = real[:, 1]
        part[slot, :, 48:64, :] = imag[:, 1]
        part[slot, :, 64:72, :] = jnp.broadcast_to(diag[None], (NQ, 8, NB))

        @pl.loop(1, NQ)
        def _(j):
            part_copy(slot, j).start()

    def end_copies(slot):
        if slot == C:
            direction, role, far_role, end, near, far = 2, 0, 1, flip, core, core
        elif slot == W:
            direction, role, far_role, end, near, far = 1, 1 - core, core, w_end, 0, 1
        else:
            direction, role, far_role, end, near, far = 1, core, 1 - core, b_end, 0, 1
        local = (direction, role, near)
        target = ends.at[direction, far_role, far]
        sem = end_recv.at[direction, far_role, far]
        copies = [
            remote(
                reduced.at[slot, 1 - core], ends.at[direction, role, near],
                end_send.at[slot, 0], end_recv.at[direction, role, near], k, sibling,
            ),
            remote(reduced.at[slot, 0], target, end_send.at[slot, 1], sem, end, 2 * q),
            remote(reduced.at[slot, 1], target, end_send.at[slot, 2], sem, end, 2 * q + 1),
        ]
        return local, copies

    def pass_on(slot):
        @pl.loop(1, NQ)
        def _(j):
            part_copy(slot, j).wait_recv()

        total = part[slot, q]
        for j in range(1, NQ):
            total = total + gathered[slot, j]
        reduced[slot, 0, 0:32, :] = total[0:32]
        reduced[slot, 0, 32:40, :] = total[64:72]
        reduced[slot, 1, 0:32, :] = total[32:64]
        reduced[slot, 1, 32:40, :] = total[64:72]
        local, copies = end_copies(slot)
        for copy in copies:
            copy.start()
        ends[local[0], local[1], local[2]] = reduced[slot, core]

    def a_piece(ref, on, h):
        if on == 0:
            return ref.at[:, 128 * h:128 * h + 128]
        return ref.at[32 * h:(32, BLOCK)[h], :]

    def a_part_copy(on, h, j):
        dest = (q + j) % NQ
        row = (4, A)[h]
        return remote(
            a_piece(part.at[A, dest], on, h), a_piece(gathered.at[A, j], on, h),
            part_send.at[row, j], part_recv.at[row, j], k, dest * 2 + core,
        )

    def a_diag(real, imag, h):
        shape = real.shape
        eye = (
            lax.broadcasted_iota(jnp.int32, shape, 0) == lax.broadcasted_iota(jnp.int32, shape, 1) + 128 * h
        )
        diag_real = jnp.sum(jnp.where(eye, real, 0.0), axis=0, keepdims=True)
        diag_imag = jnp.sum(jnp.where(eye, imag, 0.0), axis=0, keepdims=True)
        first = lax.broadcasted_iota(jnp.int32, (8, shape[1]), 0) < 4
        return jnp.broadcast_to(jnp.where(first, diag_real, diag_imag)[None], (NQ, 8, shape[1]))

    def a_hand_out(h):
        @pl.when(core == 0)
        def _():
            columns = slice(128 * h, 128 * h + 128)
            real = product[0, columns, :].T
            imag = -product[1, columns, :].T
            part[A, :, 64:72, columns] = a_diag(real, imag, h)
            real = real.reshape(NQ, 2, 16, 128)
            imag = imag.reshape(NQ, 2, 16, 128)
            for i in range(2):
                part[A, :, 32 * i:32 * i + 16, columns] = real[:, i]
                part[A, :, 32 * i + 16:32 * i + 32, columns] = imag[:, i]

            @pl.loop(1, NQ)
            def _(j):
                a_part_copy(0, h, j).start()

        @pl.when(core == 1)
        def _():
            real, imag = product[0], product[1]
            if h == 1:
                part[A, :, 64:72, :] = a_diag(real, imag, 0)
            part[A, :, 32 * h:32 * h + 16, :] = real.reshape(NQ, 2, 16, NB)[:, h]
            part[A, :, 32 * h + 16:32 * h + 32, :] = imag.reshape(NQ, 2, 16, NB)[:, h]

            @pl.loop(1, NQ)
            def _(j):
                a_part_copy(1, h, j).start()

    def a_end_copies(on, h):
        near, near_sem = ends.at[0, on, 0], end_recv.at[0, on, 0]
        far, far_sem = ends.at[0, 1 - on, 1], end_recv.at[0, 1 - on, 1]
        row = (4, A)[h]
        if on == 0:
            rows, columns = slice(0, HALF), slice(128 * h, 128 * h + 128)
            last = [(1, near, near_sem, k, sibling), (1, far, far_sem, a_end, 2 * q + 1)]
            todo = last + [(0, far, far_sem, a_end, 2 * q)]
            cuts = [(rows, columns)] * 3
        else:
            rows, columns = slice(32 * h, (32, HALF)[h]), slice(0, NB)
            todo = [(0, near, near_sem, k, sibling), (0, far, far_sem, a_end, 2 * q)]
            cuts = [(rows, columns)] * 2
            if h == 1:
                todo = todo + [(1, far, far_sem, a_end, 2 * q + 1)]
                cuts = cuts + [(slice(0, HALF), columns)]
        return [
            remote(
                reduced.at[A, half, cut[0], cut[1]], target.at[cut[0], cut[1]],
                end_send.at[row, i], sem, ka, pw,
            )
            for i, ((half, target, sem, ka, pw), cut) in enumerate(zip(todo, cuts))
        ]

    def a_pass_on(h):
        for on in range(2):
            @pl.when(core == on)
            def _():
                @pl.loop(1, NQ)
                def _(j):
                    a_part_copy(on, h, j).wait_recv()

                total = a_piece(part.at[A, q], on, h)[...]
                for j in range(1, NQ):
                    total = total + a_piece(gathered.at[A, j], on, h)[...]
                if on == 0:
                    columns = slice(128 * h, 128 * h + 128)
                    for half in range(2):
                        reduced[A, half, 0:32, columns] = total[32 * half:32 * half + 32]
                        reduced[A, half, 32:40, columns] = total[64:72]
                else:
                    reduced[A, h, 0:32, :] = total[0:32]
                    if h == 1:
                        reduced[A, 0, 32:40, :] = total[32:40]
                        reduced[A, 1, 32:40, :] = total[32:40]
                for copy in a_end_copies(on, h):
                    copy.start()

        if h == 1:
            ends[0, core, 0] = reduced[A, core]

    turn(C)
    list_copy(0).wait_recv()
    list_copy(1).start()
    for c in range(CHUNKS):
        own_copy(c, stream.at[0, :, blocks(c)]).wait_recv()
        hop_copy(1, c).start()
        pl.semaphore_wait(told.at[c], len(around))
        if c < CHUNKS - 1:
            tell(told.at[c + 1])

    turn(B)

    @pl.when(b_here)
    def _():
        @pl.loop(0, CHUNKS)
        def _(c):
            multiply(B, stream.at[0], c, core)

        hand_out(B, 1 - core)

    list_copy(1).wait_recv()
    list_copy(2).start()

    @pl.loop(0, CHUNKS)
    def _(c):
        hop_copy(1, c).wait_recv()
        hop_copy(2, c).start()

    other_copy.wait_recv()

    @pl.loop(0, CHUNKS)
    def _(c):
        multiply(C, other, c, 0)

    hand_out(C, 1)

    list_copy(2).wait_recv()
    list_copy(3).start()
    @pl.loop(0, CHUNKS)
    def _(c):
        hop_copy(2, c).wait_recv()
        hop_copy(3, c).start()

    @pl.when(w_here)
    def _():
        turn(W)

        @pl.loop(0, CHUNKS)
        def _(c):
            multiply(W, stream.at[2], c, core)

        hand_out(W, core)

    @pl.when(b_here)
    def _():
        pass_on(B)

    pass_on(C)

    list_copy(3).wait_recv()
    turn(A)

    @pl.loop(0, CHUNKS // 2)
    def _(c):
        hop_copy(3, c).wait_recv()
        multiply(A, stream.at[3], c, core)

    a_hand_out(0)

    @pl.when(w_here)
    def _():
        pass_on(W)

    @pl.loop(CHUNKS // 2, CHUNKS)
    def _(c):
        hop_copy(3, c).wait_recv()
        multiply(A, stream.at[3], c, core)

    a_hand_out(1)
    a_pass_on(0)
    a_pass_on(1)

    def arrived(direction, role, place):
        ref = ends.at[direction, role, place]
        remote(ref, ref, end_send.at[A, 0], end_recv.at[direction, role, place], k, sibling).wait_recv()

    arrived(2, 0, 1 - core)
    arrived(2, 1, 0)
    arrived(2, 1, 1)
    arrived(1, 0, 1)
    arrived(1, 1, 1)

    @pl.when(core != level // 3)
    def _():
        arrived(1, 0, 0)

    @pl.when(core != (level + 2) // 3)
    def _():
        arrived(1, 1, 0)

    arrived(0, 1 - core, 0)
    arrived(0, 0, 1)
    arrived(0, 1, 1)

    z_real = jnp.zeros((16, NB), jnp.float32)
    z_imag = jnp.zeros((16, NB), jnp.float32)
    own_column = (
        lax.broadcasted_iota(jnp.int32, (16, NB), 0) + p * 16 == lax.broadcasted_iota(jnp.int32, (16, NB), 1)
    )
    for direction in range(3):
        ahead = ends[direction, 0, 0] + ends[direction, 0, 1]
        behind = ends[direction, 1, 0] + ends[direction, 1, 1]
        real, imag = ahead[0:16], ahead[16:32]
        diag_real, diag_imag = ahead[32:33], ahead[36:37]
        corr_out[direction, 0] = real
        corr_out[direction, 1] = imag
        back_real, back_imag = behind[0:16], behind[16:32]
        row_real = jnp.sum(jnp.where(own_column, back_real, 0.0), axis=1, keepdims=True)
        row_imag = jnp.sum(jnp.where(own_column, back_imag, 0.0), axis=1, keepdims=True)
        scale = weight[direction]
        z_real += scale * (
            real * diag_real + imag * diag_imag - (back_real * row_real + back_imag * row_imag)
        )
        z_imag += scale * (
            imag * diag_real - real * diag_imag - (back_imag * row_real - back_real * row_imag)
        )
    zrows[p, 0:16, :] = z_real
    zrows[p, 16:32, :] = z_imag

    def z_copy(j):
        dest = (q + j) % NQ * 2 + core
        return remote(zrows.at[p], zrows.at[p], z_send.at[j], z_recv.at[j], k, dest)

    def z_share(j):
        owner = (q + NQ - j) % NQ * 2 + core
        return remote(zrows.at[owner], zrows.at[owner], zz_send.at[j], zz_recv.at[j], k, sibling)

    @pl.loop(1, NQ)
    def _(j):
        z_copy(j).start()

    z_share(0).start()

    @pl.loop(1, NQ)
    def _(j):
        owner = (q + NQ - j) % NQ * 2 + core
        remote(zrows.at[owner], zrows.at[owner], z_send.at[j], z_recv.at[j], k, sibling).wait_recv()
        z_share(j).start()

    @pl.loop(0, NQ)
    def _(j):
        owner = (q + NQ - j) % NQ * 2 + 1 - core
        remote(zrows.at[owner], zrows.at[owner], zz_send.at[j], zz_recv.at[j], k, sibling).wait_recv()

    real = zrows[:, 0:16, :].reshape(NB, NB)
    imag = zrows[:, 16:32, :].reshape(NB, NB)
    grad_out[0] = 0.5 * (real - real.T)
    grad_out[1] = 0.5 * (imag + imag.T)

    for h in range(HOPS):
        list_copy(h).wait_send()
    other_copy.wait_send()

    @pl.loop(0, CHUNKS)
    def _(c):
        own_copy(c, stream.at[0, :, blocks(c)]).wait_send()
        for h in range(1, HOPS):
            hop_copy(h, c).wait_send()

    def sent(slot):
        @pl.loop(1, NQ)
        def _(j):
            part_copy(slot, j).wait_send()

        for copy in end_copies(slot)[1]:
            copy.wait_send()

    for on in range(2):
        @pl.when(core == on)
        def _():
            for h in range(2):
                @pl.loop(1, NQ)
                def _(j):
                    a_part_copy(on, h, j).wait_send()

                for copy in a_end_copies(on, h):
                    copy.wait_send()

    sent(C)

    @pl.when(b_here)
    def _():
        sent(B)

    @pl.when(w_here)
    def _():
        sent(W)

    z_share(0).wait_send()

    @pl.loop(1, NQ)
    def _(j):
        z_copy(j).wait_send()
        z_share(j).wait_send()


def local(wave, wave_perm, shell_weight):
    dma = pltpu.SemaphoreType.DMA
    vmem = pl.BlockSpec(memory_space=pltpu.VMEM)
    correlation, gradient = pl.pallas_call(
        kernel,
        out_shape=(
            jax.ShapeDtypeStruct((3, 2, 16, NB), jnp.float32),
            jax.ShapeDtypeStruct((2, NB, NB), jnp.float32),
        ),
        in_specs=[pl.BlockSpec(memory_space=pl.ANY)] * 3 + [pl.BlockSpec(memory_space=pltpu.SMEM)],
        out_specs=(vmem, vmem),
        scratch_shapes=[
            pltpu.VMEM((2, 16, 16, NG), jnp.bfloat16),
            pltpu.VMEM((HOPS, 2, 16, 16, NG), jnp.bfloat16),
            pltpu.VMEM((2, 16, 16, NG), jnp.bfloat16),
            pltpu.VMEM((4, 2 * NB, NG), jnp.bfloat16),
            pltpu.VMEM((2, NB, NB), jnp.float32),
            pltpu.VMEM((HOPS + 1, 3, 1, NG), jnp.int32),
            pltpu.VMEM((4, NQ, BLOCK, NB), jnp.float32),
            pltpu.VMEM((4, NQ, BLOCK, NB), jnp.float32),
            pltpu.VMEM((4, 2, HALF, NB), jnp.float32),
            pltpu.VMEM((3, 2, 2, HALF, NB), jnp.float32),
            pltpu.VMEM((2 * NQ, 32, NB), jnp.float32),
            dma((HOPS, CHUNKS)), dma((HOPS, CHUNKS)), dma, dma, dma((HOPS,)), dma((HOPS,)),
            dma((5, NQ)), dma((5, NQ)), dma((5, 3)), dma((3, 2, 2)),
            dma((NQ,)), dma((NQ,)), dma((NQ,)), dma((NQ,)), dma, dma,
            pltpu.SemaphoreType.REGULAR((4,)),
        ],
        compiler_params=pltpu.CompilerParams(
            collective_id=0, has_side_effects=True, vmem_limit_bytes=48 * 1024 * 1024
        ),
        cost_estimate=pl.CostEstimate(
            flops=2 * 4 * 512 * NG * (NG + 512), bytes_accessed=4 * 512 * NG, transcendentals=0
        ),
    )(
        pltpu.with_memory_space_constraint(wave.reshape(2, 16, 16, NG), pltpu.HBM),
        pltpu.with_memory_space_constraint(wave.reshape(2, NQ, 2, 16, NG), pltpu.HBM),
        pltpu.with_memory_space_constraint(wave_perm[0][:, None, :], pltpu.HBM),
        pltpu.with_memory_space_constraint(shell_weight, pltpu.HBM),
    )
    return correlation[None], gradient[None]


def solution(mesh):
    placed = (P("ka", None, None, "pw"), P("ka", None, "pw"), P())
    return jax.shard_map(
        local,
        mesh=mesh,
        in_specs=placed,
        out_specs=(P("ka", None, None, "pw", None), P("ka", None, None, None)),
        check_vma=False,
    )
```

profile of v0, /device:TPU:1, one launch (start us, length us, event | category | flops | bytes accessed | tf_op | source)
XLA Modules:
  0.0 98.0 jit_solution(5741723612920607535)
XLA Ops:
  0.6 95.9 %shard_map.50 = (f32[3,2,16,256]{3,2,1,0:T(8,128)S(1)}, f32[2,256,256]{2,1,0:T(8,128)S(1)}) custom-call(bf16[2,16,16,1280]{3,2,1,0:T(8,128)(2,1)} %bitcast.7, bf16[2,8,2,16,1280]{4,3,2,1,0:T(8,128)(2,1)} %bitcast.8, s32[3,1,1280]{2,1,0:T(1,128)} %bitcast.9, f32[3]{0:T(128)} %weight.1), custom_call_target="tpu_custom_call" | custom-call | flops 9395240960 | bytes 2621440 | tf_op jit(solution)/shard_map/pallas_call | solution.py:534
  96.5 0.6 copy.7
  97.2 0.8 copy.8
where the time goes:
time: 98.1 us; the launch traced here: 98 us
  Pallas kernels  95.9 us (98%)
  local copies, waits for them, and re-layouts  1.44 us (1%)
    pallas_call x1, Pallas kernels, local(): pl.pallas_call(kernel, out_shape=(jax.ShapeDtypeStruct((3, 2, 16, NB), jn...  95.9 us

commit v1 on v0

--- a/solution.py
+++ b/solution.py
@@ -20,10 +20,10 @@
 
 
 def kernel(
-    wave_in, wave_halves, perm, weight, corr_out, grad_out,
-    wave, stream, other, turned, product, lists, part, gathered, reduced, ends, zrows,
+    wave_in, wave_halves, perm, weight_in, corr_out, grad_out,
+    weight, wave, stream, other, turned, product, lists, part, gathered, reduced, ends, zrows,
     stream_send, stream_recv, other_send, other_recv, list_send, list_recv,
-    part_send, part_recv, end_send, end_recv, z_send, z_recv, zz_send, zz_recv, wave_sem, list_sem, told,
+    part_send, part_recv, end_send, end_recv, z_send, z_recv, zz_send, zz_recv, wave_sem, list_sem, weight_sem, told,
 ):
     k = lax.axis_index("ka")
     p = lax.axis_index("pw")
@@ -49,11 +49,6 @@
             device_id=(ka, pw), device_id_type=MESH,
         )
 
-    wave_copy = pltpu.make_async_copy(wave_in, wave, wave_sem)
-    own_list_copy = pltpu.make_async_copy(perm, lists.at[0], list_sem)
-    wave_copy.start()
-    own_list_copy.start()
-
     around = [
         ((k + 2) % NK, p), ((k + 30) % NK, p), (flip, p), (flip, (q + 4) % NQ * 2 + core),
         (k, (q // 4 * 4 + (q + 1) % 4) * 2 + core), (k, (q // 4 * 4 + (q + 3) % 4) * 2 + core), (k, sibling),
@@ -65,6 +60,12 @@
 
     barrier = pltpu.get_barrier_semaphore()
     tell(barrier)
+    wave_copy = pltpu.make_async_copy(wave_in, wave, wave_sem)
+    own_list_copy = pltpu.make_async_copy(perm, lists.at[0], list_sem)
+    weight_copy = pltpu.make_async_copy(weight_in, weight, weight_sem)
+    wave_copy.start()
+    own_list_copy.start()
+    weight_copy.start()
     pl.semaphore_wait(barrier, len(around))
 
     def blocks(c):
@@ -106,38 +107,32 @@
     tell(told.at[0])
     own_list_copy.wait()
     wave_copy.wait()
-
-    def turn(slot):
-        which = (1 - core) * 3 * (slot // 2) * (1 - slot % 2) + core * (4 - 3 * slot) * (1 - slot // 2)
-        direction = (slot + 1) // 2
-        at_start = (1 - core) * (1 - slot // 2 * (1 - slot % 2)) + core * (slot // 2)
-
-        @pl.when(at_start == 1)
-        def _():
-            @pl.loop(0, NG // 256)
-            def _(j):
-                row = lists[which, direction] - p * NG
-                wanted = lax.broadcasted_iota(jnp.int32, (256, NG), 0) + j * 256
-                pick = jnp.where(wanted == row, 1.0, 0.0).astype(jnp.bfloat16)
-                value = lax.dot_general(
-                    wave[...].reshape(2 * NB, NG), pick, (((1,), (1,)), ((), ())),
-                    preferred_element_type=jnp.float32,
-                )
-                turned[slot, :, pl.ds(pl.multiple_of(j * 256, 256), 256)] = value.astype(jnp.bfloat16)
-
-        @pl.when(at_start == 0)
-        def _():
-            @pl.loop(0, NG // 256)
-            def _(j):
-                columns = pl.ds(pl.multiple_of(j * 256, 256), 256)
-                row = lists[which, direction, :, columns] - p * NG
-                held = lax.broadcasted_iota(jnp.int32, (NG, 256), 0)
-                pick = jnp.where(held == row, 1.0, 0.0).astype(jnp.bfloat16)
-                value = lax.dot_general(
-                    wave[...].reshape(2 * NB, NG), pick, (((1,), (0,)), ((), ())),
-                    preferred_element_type=jnp.float32,
-                )
-                turned[slot, :, columns] = value.astype(jnp.bfloat16)
+    weight_copy.wait()
+
+    def turn_start(slot, direction):
+        @pl.loop(0, NG // 256)
+        def _(j):
+            row = lists[0, direction] - p * NG
+            wanted = lax.broadcasted_iota(jnp.int32, (256, NG), 0) + j * 256
+            pick = jnp.where(wanted == row, 1.0, 0.0).astype(jnp.bfloat16)
+            value = lax.dot_general(
+                wave[...].reshape(2 * NB, NG), pick, (((1,), (1,)), ((), ())),
+                preferred_element_type=jnp.float32,
+            )
+            turned[slot, :, pl.ds(pl.multiple_of(j * 256, 256), 256)] = value.astype(jnp.bfloat16)
+
+    def turn_end(slot, direction, hops):
+        @pl.loop(0, NG // 256)
+        def _(j):
+            columns = pl.ds(pl.multiple_of(j * 256, 256), 256)
+            row = lists[hops, direction, :, columns] - p * NG
+            held = lax.broadcasted_iota(jnp.int32, (NG, 256), 0)
+            pick = jnp.where(held == row, 1.0, 0.0).astype(jnp.bfloat16)
+            value = lax.dot_general(
+                wave[...].reshape(2 * NB, NG), pick, (((1,), (0,)), ((), ())),
+                preferred_element_type=jnp.float32,
+            )
+            turned[slot, :, columns] = value.astype(jnp.bfloat16)
 
     def multiply(slot, source, c, order):
         value = lax.dot_general(
@@ -322,7 +317,7 @@
         if h == 1:
             ends[0, core, 0] = reduced[A, core]
 
-    turn(C)
+    turn_start(C, 2)
     list_copy(0).wait_recv()
     list_copy(1).start()
     for c in range(CHUNKS):
@@ -332,10 +327,16 @@
         if c < CHUNKS - 1:
             tell(told.at[c + 1])
 
-    turn(B)
-
     @pl.when(b_here)
     def _():
+        @pl.when(core == 0)
+        def _():
+            turn_start(B, 1)
+
+        @pl.when(core == 1)
+        def _():
+            turn_end(B, 1, 1)
+
         @pl.loop(0, CHUNKS)
         def _(c):
             multiply(B, stream.at[0], c, core)
@@ -344,6 +345,10 @@
 
     list_copy(1).wait_recv()
     list_copy(2).start()
+
+    @pl.when(core == 0)
+    def _():
+        turn_start(A, 0)
 
     @pl.loop(0, CHUNKS)
     def _(c):
@@ -360,6 +365,16 @@
 
     list_copy(2).wait_recv()
     list_copy(3).start()
+
+    @pl.when(w_here)
+    def _():
+        @pl.when(core == 0)
+        def _():
+            turn_end(W, 1, 3)
+
+        @pl.when(core == 1)
+        def _():
+            turn_start(W, 1)
     @pl.loop(0, CHUNKS)
     def _(c):
         hop_copy(2, c).wait_recv()
@@ -367,22 +382,19 @@
 
     @pl.when(w_here)
     def _():
-        turn(W)
-
         @pl.loop(0, CHUNKS)
         def _(c):
             multiply(W, stream.at[2], c, core)
 
         hand_out(W, core)
 
-    @pl.when(b_here)
-    def _():
-        pass_on(B)
-
     pass_on(C)
 
     list_copy(3).wait_recv()
-    turn(A)
+
+    @pl.when(core == 1)
+    def _():
+        turn_end(A, 0, 4)
 
     @pl.loop(0, CHUNKS // 2)
     def _(c):
@@ -391,16 +403,21 @@
 
     a_hand_out(0)
 
-    @pl.when(w_here)
-    def _():
-        pass_on(W)
-
     @pl.loop(CHUNKS // 2, CHUNKS)
     def _(c):
         hop_copy(3, c).wait_recv()
         multiply(A, stream.at[3], c, core)
 
     a_hand_out(1)
+
+    @pl.when(b_here)
+    def _():
+        pass_on(B)
+
+    @pl.when(w_here)
+    def _():
+        pass_on(W)
+
     a_pass_on(0)
     a_pass_on(1)
 
@@ -537,9 +554,10 @@
             jax.ShapeDtypeStruct((3, 2, 16, NB), jnp.float32),
             jax.ShapeDtypeStruct((2, NB, NB), jnp.float32),
         ),
-        in_specs=[pl.BlockSpec(memory_space=pl.ANY)] * 3 + [pl.BlockSpec(memory_space=pltpu.SMEM)],
+        in_specs=[pl.BlockSpec(memory_space=pl.ANY)] * 4,
         out_specs=(vmem, vmem),
         scratch_shapes=[
+            pltpu.SMEM((3,), jnp.float32),
             pltpu.VMEM((2, 16, 16, NG), jnp.bfloat16),
             pltpu.VMEM((HOPS, 2, 16, 16, NG), jnp.bfloat16),
             pltpu.VMEM((2, 16, 16, NG), jnp.bfloat16),
@@ -554,7 +572,7 @@
             dma((HOPS, CHUNKS)), dma((HOPS, CHUNKS)), dma, dma, dma((HOPS,)), dma((HOPS,)),
             dma((5, NQ)), dma((5, NQ)), dma((5, 3)), dma((3, 2, 2)),
             dma((NQ,)), dma((NQ,)), dma((NQ,)), dma((NQ,)), dma, dma,
-            pltpu.SemaphoreType.REGULAR((4,)),
+            dma, pltpu.SemaphoreType.REGULAR((4,)),
         ],
         compiler_params=pltpu.CompilerParams(
             collective_id=0, has_side_effects=True, vmem_limit_bytes=48 * 1024 * 1024

time: 98.1 us -> 96.6 us (0.985)
  Pallas kernels: 95.9 us -> 94.4 us
    pallas_call x1, Pallas kernels: 95.9 us -> 94.4 us  [local(): pl.pallas_call(kernel, out_shape=(jax.ShapeDtypeStruct((3, 2, 16, NB), jn...]
where the time goes in v1:
time: 96.6 us; the launch traced here: 96.5 us
  Pallas kernels  94.4 us (98%)
  local copies, waits for them, and re-layouts  1.44 us (1%)
    pallas_call x1, Pallas kernels, local(): pl.pallas_call(kernel, out_shape=(jax.ShapeDtypeStruct((3, 2, 16, NB), jn...  94.4 us

profile of v1, /device:TPU:1, one launch (start us, length us, event | category | flops | bytes accessed | tf_op | source)
XLA Modules:
  0.0 96.5 jit_solution(15059546331462617083)
XLA Ops:
  0.6 94.4 %shard_map.50 = (f32[3,2,16,256]{3,2,1,0:T(8,128)S(1)}, f32[2,256,256]{2,1,0:T(8,128)S(1)}) custom-call(bf16[2,16,16,1280]{3,2,1,0:T(8,128)(2,1)} %bitcast.7, bf16[2,8,2,16,1280]{4,3,2,1,0:T(8,128)(2,1)} %bitcast.8, s32[3,1,1280]{2,1,0:T(1,128)} %bitcast.9, f32[3]{0:T(128)} %weight_in.1), custom_call_target="tpu_custom_call" | custom-call | flops 9395240960 | bytes 2621440 | tf_op jit(solution)/shard_map/pallas_call | solution.py:551
  95.0 0.6 copy.7
  95.7 0.8 copy.8

commit v2 on v1

--- a/solution.py
+++ b/solution.py
@@ -85,8 +85,9 @@
 
     def list_copy(h):
         source = perm if h == 0 else lists.at[h]
+        rows = slice(0, 1 if h == HOPS - 1 else 2)
         return remote(
-            source.at[0:2], lists.at[h + 1, 0:2], list_send.at[h], list_recv.at[h], to_next, p
+            source.at[rows], lists.at[h + 1, rows], list_send.at[h], list_recv.at[h], to_next, p
         )
 
     other_copy = remote(wave_in, other, other_send, other_recv, flip, p)
@@ -410,6 +411,8 @@
 
     a_hand_out(1)
 
+    a_pass_on(0)
+
     @pl.when(b_here)
     def _():
         pass_on(B)
@@ -418,7 +421,6 @@
     def _():
         pass_on(W)
 
-    a_pass_on(0)
     a_pass_on(1)
 
     def arrived(direction, role, place):

time: 96.6 us -> 96.5 us (level)
  no operation moved by 1% of the time
where the time goes in v2:
time: 96.5 us; the launch traced here: 96.4 us
  Pallas kernels  94.3 us (98%)
  local copies, waits for them, and re-layouts  1.44 us (1%)
    pallas_call x1, Pallas kernels, local(): pl.pallas_call(kernel, out_shape=(jax.ShapeDtypeStruct((3, 2, 16, NB), jn...  94.3 us

profile of v2, /device:TPU:1, one launch (start us, length us, event | category | flops | bytes accessed | tf_op | source)
XLA Modules:
  0.0 96.4 jit_solution(9423131978788624905)
XLA Ops:
  0.6 94.3 %shard_map.50 = (f32[3,2,16,256]{3,2,1,0:T(8,128)S(1)}, f32[2,256,256]{2,1,0:T(8,128)S(1)}) custom-call(bf16[2,16,16,1280]{3,2,1,0:T(8,128)(2,1)} %bitcast.7, bf16[2,8,2,16,1280]{4,3,2,1,0:T(8,128)(2,1)} %bitcast.8, s32[3,1,1280]{2,1,0:T(1,128)} %bitcast.9, f32[3]{0:T(128)} %weight_in.1), custom_call_target="tpu_custom_call" | custom-call | flops 9395240960 | bytes 2621440 | tf_op jit(solution)/shard_map/pallas_call | solution.py:553
  95.0 0.6 copy.7
  95.6 0.8 copy.8
